TPU v7x, 32 devices: a whole 2x2x4 slice. The times are simulated.
32 devices in a mesh: lag: 16 (over z, y, x), space: 2 (over core).
Axes of the slice: x: 2, y: 2, z: 4, core: 2. Of those that a mesh axis runs over, the one named last changes fastest.
Arguments:
- ensemble: bfloat16 [16, 256, 1024], P('lag', 'space'), may hold values from -6 to 6
- slot_order: int32 [16], replicated, may hold values from 0 to 15, each once
- neighbour_shift: int32 [6, 256], P(None, 'space'), may hold values from -16 to 16, as said below
- edge_coupling: float32 [6, 256], P(None, 'space'), may hold values from 0.02 to 0.15
- observation_cells: int32 [2, 4, 32], P(None, None, 'space'), may hold values from 0 to 127
- observation_weight: float32 [2, 4, 32], P(None, None, 'space'), may hold values from 0.1 to 0.6
- observation_reading: float32 [2, 32], P(None, 'space'), may hold values from -6 to 6
- observation_variance: float32 [2, 32], replicated, may hold values from 0.25 to 2
- observation_jitter: float32 [2, 32, 1024], P(None, 'space'), may hold values from -6 to 6
Outputs:
- analysed: bfloat16 [16, 256, 1024], P('lag', 'space')
- retired: bfloat16 [2, 1024, 256], P(None, 'lag', 'space')
Inputs may be any that keep to these rules, and one draw needn't show every extreme that they name: `neighbour_shift`: for each cell the 6 offsets are distinct and nonzero. `observation_cells`: observation p reads cells of the partition of 128 cells numbered p // 16.
All inputs are finite; a program needn't handle non-finite values.
Results may differ from a plain program's by a relative error of at most 0.0054.
Values may be sent and summed in bfloat16 or wider, within the bound.
A program may use at most 64 MiB of HBM per device.

v0:
```python
import jax
import jax.numpy as jnp
from jax import lax
from jax.sharding import PartitionSpec as P

HALO = 16
FC_STEPS = 4
CYCLES = 2


def padded_2(cells, sides, width):
    for axis, dim in sides:
        count = lax.axis_size(axis)
        ends = count - 1
        head = lax.slice_in_dim(cells, 0, width, axis=dim)
        tail = lax.slice_in_dim(cells, cells.shape[dim] - width, cells.shape[dim], axis=dim)
        cells = jnp.concatenate(
            [
                lax.ppermute(tail, axis, [(i, (i + 1) % count) for i in range(ends)]),
                cells,
                lax.ppermute(head, axis, [((i + 1) % count, i) for i in range(ends)]),
            ],
            axis=dim,
        )
    return cells


def spread_2(value, axis, source):
    kept = jnp.where(lax.axis_index(axis) == source, value, 0).astype(value.dtype)
    return lax.psum(kept, axis)


def relax_once(padded, centre, offsets, coefficients, lead_rows):
    anchor = jnp.arange(centre.shape[0], dtype=jnp.int32) + lead_rows
    accrued = jnp.zeros_like(centre)
    for neighbour in range(offsets.shape[0]):
        picked = jnp.clip(anchor + offsets[neighbour], 0, padded.shape[0] - 1)
        accrued = accrued + coefficients[neighbour][:, None] * (padded[picked] - centre)
    return centre + accrued


def step_forward(present_state, offsets, coefficients):
    field_f = present_state.astype(jnp.float32)
    for repeat in range(FC_STEPS):
        padded = padded_2(field_f, (("space", 0),), HALO)
        field_f = relax_once(padded, field_f, offsets, coefficients, HALO)
    return field_f.astype(jnp.bfloat16)


def observe_local(
    predict_ahead, vertex_list, vertex_weights, observation_readings, variance_total, random_jitter
):
    per_device = vertex_list.shape[1]
    to_single_float = predict_ahead.astype(jnp.float32)
    measured = jnp.zeros((per_device, to_single_float.shape[1]), jnp.float32)
    for corner in range(vertex_list.shape[0]):
        measured = measured + vertex_weights[corner][:, None] * to_single_float[vertex_list[corner]]
    centre = jnp.mean(measured, axis=1, keepdims=True)
    spread = (measured - centre).astype(jnp.bfloat16)
    variance_own = lax.dynamic_slice_in_dim(
        variance_total, lax.axis_index("space") * per_device, per_device
    )
    innovation = (
        observation_readings[:, None] + jnp.sqrt(variance_own)[:, None] * random_jitter - measured
    ).astype(jnp.bfloat16)
    return (spread, innovation)


def solve_weights(spread, innovation, variance_total):
    spread_all, innovation_all = (
        lax.all_gather(spread, "space", axis=0, tiled=True),
        lax.all_gather(innovation, "space", axis=0, tiled=True),
    )
    gram_matrix = lax.dot_general(
        spread_all, spread_all, (((1,), (1,)), ((), ())), preferred_element_type=jnp.float32
    )
    gram_matrix = gram_matrix + jnp.diag((spread.shape[1] - 1) * variance_total)
    factor = jnp.linalg.cholesky(gram_matrix)
    solved = jax.scipy.linalg.cho_solve((factor, True), innovation_all.astype(jnp.float32)).astype(
        jnp.bfloat16
    )
    product = lax.dot_general(
        spread_all, solved, (((0,), (0,)), ((), ())), preferred_element_type=jnp.float32
    )
    return product.astype(jnp.bfloat16)


def assimilate_window(present_state, gain_weights):
    values = present_state.astype(jnp.float32)
    centre = jnp.mean(values, axis=1, keepdims=True)
    spread = (values - centre).astype(jnp.bfloat16)
    return (values + jnp.dot(spread, gain_weights, preferred_element_type=jnp.float32)).astype(
        jnp.bfloat16
    )


def on_device(
    ensemble,
    slot_order,
    neighbour_shift,
    edge_coupling,
    observation_cells,
    observation_weight,
    observation_reading,
    observation_variance,
    observation_jitter,
):
    present_state = ensemble[0]
    members = present_state.shape[1]
    slab_count = lax.axis_size("lag")
    lag_rank = lax.axis_index("lag")
    member_rows = members // slab_count
    departed = []
    for cycle_number in range(CYCLES):
        forcing_term = slot_order[(slab_count - cycle_number) % slab_count]
        target = slot_order[(slab_count - 1 - cycle_number) % slab_count]
        variance_total = observation_variance[cycle_number]
        newest = spread_2(present_state, "lag", forcing_term)
        predict_ahead = step_forward(newest, neighbour_shift, edge_coupling)
        spread, innovation = observe_local(
            predict_ahead,
            observation_cells[cycle_number],
            observation_weight[cycle_number],
            observation_reading[cycle_number],
            variance_total,
            observation_jitter[cycle_number],
        )
        gain_weights = solve_weights(spread, innovation, variance_total)
        refreshed_state = assimilate_window(predict_ahead, gain_weights)
        updated = assimilate_window(present_state, gain_weights)
        outgoing = spread_2(updated, "lag", target)
        member_block = lax.dynamic_slice_in_dim(outgoing, lag_rank * member_rows, member_rows, 1)
        departed.append(member_block.T)
        present_state = jnp.where(lag_rank == target, refreshed_state, updated)
    return (present_state[None], jnp.stack(departed))


def solution(mesh):
    in_specs = (
        P("lag", "space", None),
        P(),
        P(None, "space"),
        P(None, "space"),
        P(None, None, "space"),
        P(None, None, "space"),
        P(None, "space"),
        P(),
        P(None, "space", None),
    )
    out_specs = (P("lag", "space", None), P(None, "lag", "space"))
    return jax.shard_map(
        on_device, mesh=mesh, in_specs=in_specs, out_specs=out_specs, check_vma=False
    )
```

profile of v0, /device:TPU:1, one launch (start us, length us, event | category | flops | bytes accessed | tf_op | source)
XLA Modules:
  0.0 493.1 jit_solution(4502298590233057489)
XLA Ops:
  7.2 1.4 fusion.90
  11.2 1.4 multiply_bitcast_fusion
  12.5 1.3 slice_bitcast_fusion.5
  14.7 1.5 fusion.72
  16.2 1.5 slice_bitcast_fusion.4
  19.0 1.5 slice_bitcast_fusion.15
  20.5 100.3 %all-reduce.5.cloned.1.call-done = bf16[128,1024]{1,0:T(8,128)(2,1)} async-done(((bf16[128,1024]{1,0:T(8,128)(2,1)}), bf16[128,1024]{1,0:T(8,128)(2,1)}) %all-reduce.5.cloned.1.call-update) | async-done | bytes 262160 | tf_op jit(solution)/shard_map/psum | solution.py:30
  121.6 4.4 collective-permute-start.1
  126.0 1.3 collective-permute-start
  133.4 1.9 gather_fusion.5
  135.2 1.5 convert_add_fusion.1
  136.7 2.8 collective-permute-start.3
  139.5 1.3 collective-permute-start.2
  140.9 1.8 collective-permute-done.2
  145.5 1.6 gather_fusion.8
  147.1 1.6 gather_fusion.7
  148.7 1.6 gather_fusion.6
  150.3 1.8 add_add_fusion.3
  152.1 2.1 collective-permute-start.5
  154.1 1.3 collective-permute-start.4
  155.5 1.8 collective-permute-done.4
  160.0 1.6 gather_fusion.14
  161.6 1.6 gather_fusion.13
  163.2 1.6 gather_fusion.12
  164.8 1.8 add_add_fusion.2
  166.6 2.1 collective-permute-start.7
  168.6 1.3 collective-permute-start.6
  174.5 1.6 gather_fusion.20
  176.1 1.6 gather_fusion.19
  177.7 1.6 gather_fusion.18
  179.3 2.0 convert_reduce_fusion.3
  184.1 1.8 all_gather.12
  185.9 2.0 all_gather.13
  188.2 2.9 cholesky.44
  192.4 2.4 custom-call.8
  197.5 1.3 broadcast_select_fusion.1
  199.4 103.0 %all-reduce.7.cloned.1.call-done = bf16[128,1024]{1,0:T(8,128)(2,1)} async-done(((bf16[128,1024]{1,0:T(8,128)(2,1)}), bf16[128,1024]{1,0:T(8,128)(2,1)}) %all-reduce.7.cloned.1.call-update) | async-done | bytes 262160 | tf_op jit(solution)/shard_map/psum | solution.py:30
  303.1 4.4 collective-permute-start.9
  307.5 1.3 collective-permute-start.8
  314.9 1.7 gather_fusion.33
  316.6 1.5 convert_add_fusion
  318.2 2.8 collective-permute-start.11
  321.0 1.3 collective-permute-start.10
  322.9 1.2 collective-permute-done.10
  327.9 1.7 gather_fusion.35
  329.6 1.7 gather_fusion.34
  331.3 1.6 add_add_fusion.1
  333.0 2.1 collective-permute-start.13
  335.1 1.3 collective-permute-start.12
  342.0 1.7 gather_fusion.41
  343.7 1.7 gather_fusion.40
  345.4 1.6 add_add_fusion
  347.0 2.1 collective-permute-start.15
  349.1 1.5 collective-permute-start.14
  350.7 1.6 collective-permute-done.14
  355.1 1.7 gather_fusion.48
  356.8 1.7 gather_fusion.47
  358.5 1.8 gather_fusion.46
  360.4 2.0 convert_reduce_fusion.2
  365.7 1.8 all_gather.14
  367.5 1.8 all_gather.15
  369.6 2.9 cholesky.55
  373.9 2.4 custom-call.9
  380.1 104.1 %all-reduce.9.cloned.1.call-done = (bf16[128,1024]{1,0:T(8,128)(2,1)}, bf16[128,1024]{1,0:T(8,128)(2,1)}) async-done(((bf16[128,1024]{1,0:T(8,128)(2,1)}, bf16[128,1024]{1,0:T(8,128)(2,1)}), (bf16[128,1024]{1,0:T(8,128)(2,1)}, bf16[128,1024]{1,0:T(8,128)(2,1)})) %all-reduce.9.cloned.1.call-update) | async-done | bytes 524304 | tf_op jit(solution)/shard_map/psum | solution.py:30
  (207 shorter events, 57.6 us)
Async XLA Ops:
  7.2 113.6 %all-reduce.5.cloned.1.call-start = ((), (), s32[]{:S(2)}) async-start(), calls=%async_computation | async-start | bytes 524288 | tf_op jit(solution)/shard_map/psum | solution.py:30
  10.0 292.3 %all-reduce.7.cloned.1.call-start = ((), (), s32[]{:S(2)}) async-start(), calls=%async_computation.1 | async-start | bytes 524288 | tf_op jit(solution)/shard_map/psum | solution.py:30
  18.3 111.7 %copy-start.8 = (s32[1024]{0:T(1024)}, s32[1024]{0:T(1024)S(1)}, u32[]{:S(2)}) copy-start(s32[1024]{0:T(1024)S(1)} %get-tuple-element.82) | copy-start | bytes 12292
  18.3 111.7 %copy-start.10 = (s32[1024]{0:T(1024)}, s32[1024]{0:T(1024)S(1)}, u32[]{:S(2)}) copy-start(s32[1024]{0:T(1024)S(1)} %get-tuple-element.81) | copy-start | bytes 12292
  18.3 112.5 %copy-start.12 = (s32[1024]{0:T(1024)}, s32[1024]{0:T(1024)S(1)}, u32[]{:S(2)}) copy-start(s32[1024]{0:T(1024)S(1)} %get-tuple-element.80) | copy-start | bytes 12292
  18.3 113.3 %copy-start.14 = (s32[1024]{0:T(1024)}, s32[1024]{0:T(1024)S(1)}, u32[]{:S(2)}) copy-start(s32[1024]{0:T(1024)S(1)} %get-tuple-element.79) | copy-start | bytes 12292
  121.6 7.3 %collective-permute-start.1 = (f32[16,1024]{1,0:T(8,128)S(1)}, f32[16,1024]{1,0:T(8,128)S(1)}, u32[]{:S(2)}, u32[]{:S(2)}) collective-permute-start(f32[16,1024]{1,0:T(8,128)S(1)} %get-tuple-element.31), channel_id=1, source_target_pairs={{1,0},{3,2},{5,4},{7,6},{9,8},{11,10},{13,12},{15,14},{17,16},{19,... | collective-permute-start | bytes 196616 | tf_op jit(solution)/shard_map/ppermute | solution.py:21
  126.0 3.1 collective-permute-start
  133.4 1.9 copy-start.1
  135.2 5.6 %copy-start.35 = (s32[16]{0:T(128)S(1)}, s32[16]{0:T(128)}, u32[]{:S(2)}) copy-start(s32[16]{0:T(128)} %get-tuple-element.42) | copy-start | bytes 196
  135.2 5.6 %copy-start.36 = (s32[16]{0:T(128)S(1)}, s32[16]{0:T(128)}, u32[]{:S(2)}) copy-start(s32[16]{0:T(128)} %get-tuple-element.43) | copy-start | bytes 196
  136.7 4.2 collective-permute-start.3
  139.5 3.1 collective-permute-start.2
  143.7 0.9 copy-start.15
  144.6 0.8 copy-start.13
  145.5 1.6 copy-start.11
  147.1 1.6 copy-start.9
  148.7 1.6 copy-start.4
  148.7 1.6 copy-start.6
  150.2 5.2 %copy-start.33 = (s32[16]{0:T(128)S(1)}, s32[16]{0:T(128)}, u32[]{:S(2)}) copy-start(s32[16]{0:T(128)} %get-tuple-element.44) | copy-start | bytes 196
  150.2 5.2 %copy-start.34 = (s32[16]{0:T(128)S(1)}, s32[16]{0:T(128)}, u32[]{:S(2)}) copy-start(s32[16]{0:T(128)} %get-tuple-element.45) | copy-start | bytes 196
  152.1 3.4 collective-permute-start.5
  154.1 3.1 collective-permute-start.4
  164.8 5.2 %copy-start.37 = (f32[1,32]{1,0:T(1,128)S(1)}, f32[1,32]{1,0:T(1,128)}, u32[]{:S(2)}) copy-start(f32[1,32]{1,0:T(1,128)} %get-tuple-element.62) | copy-start | bytes 388
  164.8 5.2 %copy-start.38 = (f32[1,32]{1,0:T(1,128)S(1)}, f32[1,32]{1,0:T(1,128)}, u32[]{:S(2)}) copy-start(f32[1,32]{1,0:T(1,128)} %get-tuple-element.63) | copy-start | bytes 388
  166.6 4.1 collective-permute-start.7
  168.6 3.1 collective-permute-start.6
  181.2 2.5 copy-start.2
  181.2 2.5 copy-start.21
  181.2 2.5 copy-start.22
  181.3 2.5 copy-start.23
  181.3 2.5 copy-start.24
  181.3 2.5 copy-start.28
  181.3 6.7 %copy-start.27 = (f32[32]{0:T(128)S(1)}, f32[32]{0:T(128)}, u32[]{:S(2)}) copy-start(f32[32]{0:T(128)} %get-tuple-element.61) | copy-start | bytes 388
  183.1 13.1 %copy-start = (bf16[1,128,1024]{2,1,0:T(8,128)(2,1)S(1)}, bf16[1,128,1024]{2,1,0:T(8,128)(2,1)}, u32[]{:S(2)}) copy-start(bf16[1,128,1024]{2,1,0:T(8,128)(2,1)} %param.12) | copy-start | bytes 786436
  183.1 13.1 %copy-start.40 = (f32[128]{0:T(128)S(1)}, f32[128]{0:T(128)}, u32[]{:S(2)}) copy-start(f32[128]{0:T(128)} %broadcast_multiply_fusion.4) | copy-start | bytes 1540
  197.5 111.4 %copy-start.31 = (s32[16]{0:T(128)S(1)}, s32[16]{0:T(128)}, u32[]{:S(2)}) copy-start(s32[16]{0:T(128)} %get-tuple-element.46) | copy-start | bytes 196
  197.5 111.4 %copy-start.32 = (s32[16]{0:T(128)S(1)}, s32[16]{0:T(128)}, u32[]{:S(2)}) copy-start(s32[16]{0:T(128)} %get-tuple-element.47) | copy-start | bytes 196
  198.8 285.4 %all-reduce.9.cloned.1.call-start = ((), (), s32[]{:S(2)}) async-start(), calls=%async_computation.2 | async-start | bytes 1048576 | tf_op jit(solution)/shard_map/psum | solution.py:30
  303.1 7.3 %collective-permute-start.9 = (f32[16,1024]{1,0:T(8,128)S(1)}, f32[16,1024]{1,0:T(8,128)S(1)}, u32[]{:S(2)}, u32[]{:S(2)}) collective-permute-start(f32[16,1024]{1,0:T(8,128)S(1)} %get-tuple-element.29), channel_id=1, source_target_pairs={{1,0},{3,2},{5,4},{7,6},{9,8},{11,10},{13,12},{15,14},{17,16},{19,... | collective-permute-start | bytes 196616 | tf_op jit(solution)/shard_map/ppermute | solution.py:21
  307.5 3.1 collective-permute-start.8
  316.6 5.7 %copy-start.29 = (s32[16]{0:T(128)S(1)}, s32[16]{0:T(128)}, u32[]{:S(2)}) copy-start(s32[16]{0:T(128)} %get-tuple-element.40) | copy-start | bytes 196
  316.6 5.7 %copy-start.30 = (s32[16]{0:T(128)S(1)}, s32[16]{0:T(128)}, u32[]{:S(2)}) copy-start(s32[16]{0:T(128)} %get-tuple-element.41) | copy-start | bytes 196
  318.2 4.8 collective-permute-start.11
  321.0 3.1 collective-permute-start.10
  333.0 4.0 collective-permute-start.13
  335.1 3.1 collective-permute-start.12
  345.4 5.2 %copy-start.39 = (f32[128]{0:T(128)S(1)}, f32[128]{0:T(128)}, u32[]{:S(2)}) copy-start(f32[128]{0:T(128)} %convert_reduce_fusion) | copy-start | bytes 1540
  347.0 3.6 collective-permute-start.15
  349.1 3.1 collective-permute-start.14
  358.5 1.8 copy-start.5
  358.5 1.8 copy-start.7
  362.3 3.0 copy-start.3
  362.3 3.0 copy-start.16
  362.4 3.0 copy-start.17
  362.4 3.0 copy-start.18
  362.4 3.0 copy-start.19
  362.4 3.0 copy-start.20
  362.4 3.0 copy-start.26
  362.4 7.0 %copy-start.25 = (f32[32]{0:T(128)S(1)}, f32[32]{0:T(128)}, u32[]{:S(2)}) copy-start(f32[32]{0:T(128)} %get-tuple-element.60) | copy-start | bytes 388
Sparse Core Ops, SparseCore 0:
  13.8 106.9 all-reduce.4
  198.9 103.3 all-reduce.6
  379.0 105.1 all-reduce.8
where the time goes:
time: 497 us; the launch traced here: 493 us
  waiting for transfers between devices  317 us (64%)
  local copies, waits for them, and re-layouts  72.2 us (15%)
  other arithmetic  38.9 us (8%)
  starting transfers between devices  33.4 us (7%)
  between operations  16.7 us (3%)
  matrix products  7.82 us (2%)
  blocking collectives  7.55 us (2%)
    psum x3, waiting for transfers between devices, spread_2(): return lax.psum(kept, axis)  307 us
    gather x48, local copies, waits for them, and re-layouts, relax_once(): padded[picked] - centre  56.3 us
    ppermute x8, starting transfers between devices, padded_2(): lax.ppermute(head, axis, [((i + 1) % count, i) for i in range(ends)])  22.7 us
    ppermute x8, starting transfers between devices, padded_2(): lax.ppermute(tail, axis, [(i, (i + 1) % count) for i in range(ends)])  10.6 us
  transfers between devices with their start and end apart: 19, of which 11 were waited for; matrix products, arithmetic and copies ran while one was open for 3% of the time, Pallas kernels for 0%

commit v1 on v0

v1 whole, which is shorter than its diff:
```python
import functools
import jax
import jax.numpy as jnp
from jax import lax
from jax.experimental import pallas as pl
from jax.experimental.pallas import tpu as pltpu
from jax.sharding import PartitionSpec as P

FC_STEPS = 4
LANES = 128
MESH = pl.DeviceIdType.MESH
VMEM_BYTES = 50 * 1024 * 1024
F32 = jnp.float32
BF16 = jnp.bfloat16


def exchange_kernel(lags, spaces, slot_ref, slab_ref, *refs):
    small_count = (len(refs) - 10) // 2
    small_in, refs = refs[:small_count], refs[small_count:]
    whole_ref, refs = refs[0], refs[1:]
    small_out, refs = refs[:small_count], refs[small_count:]
    landing, chosen, send_1, recv_1, send_2, recv_2, send_3, recv_3, sems_small = refs
    send_s, recv_s = sems_small.at[0], sems_small.at[1]
    lag, space = lax.axis_index("lag"), lax.axis_index("space")
    cells, members = slab_ref.shape
    across = members // LANES
    rows = cells * across // lags

    def place(block):
        return (
            pl.ds(pl.multiple_of((block // across) * rows, rows), rows),
            pl.ds(pl.multiple_of((block % across) * LANES, LANES), LANES),
        )

    def lag_at(step):
        return lax.rem(lag + step, lags)

    def space_at(step):
        return lax.rem(space + step, spaces)

    barrier = pltpu.get_barrier_semaphore()
    for step in range(1, lags):
        pl.semaphore_signal(barrier, inc=1, device_id=(lag_at(step), space), device_id_type=MESH)
    for step in range(1, spaces):
        pl.semaphore_signal(barrier, inc=1, device_id=(lag, space_at(step)), device_id_type=MESH)
    pl.semaphore_wait(barrier, lags - 1 + spaces - 1)

    scatter = []
    for step in range(1, lags):
        copy = pltpu.make_async_remote_copy(
            src_ref=slab_ref.at[place(lag_at(step))],
            dst_ref=landing.at[step],
            send_sem=send_1.at[step],
            recv_sem=recv_1.at[step],
            device_id=(lag_at(step), space),
            device_id_type=MESH,
        )
        copy.start()
        scatter.append(copy)
    small = []
    for step in range(1, spaces):
        for item in range(small_count):
            copy = pltpu.make_async_remote_copy(
                src_ref=small_in[item],
                dst_ref=small_out[item].at[space],
                send_sem=send_s.at[item, step],
                recv_sem=recv_s.at[item, step],
                device_id=(lag, space_at(step)),
                device_id_type=MESH,
            )
            copy.start()
            small.append(copy)
    for item in range(small_count):
        small_out[item][space] = small_in[item][...]
    source = slot_ref[0]
    block = jnp.where(lag == source, slab_ref[place(lag)], jnp.zeros((rows, LANES), BF16))
    for step in range(1, lags):
        scatter[step - 1].wait_recv()
        block = jnp.where(lag_at(lags - step) == source, landing[step], block)
    chosen[...] = block
    whole_ref[(space,) + place(lag)] = block
    gather = []
    for step in range(1, lags):
        copy = pltpu.make_async_remote_copy(
            src_ref=chosen,
            dst_ref=whole_ref.at[(space,) + place(lag)],
            send_sem=send_2.at[step],
            recv_sem=recv_2.at[step],
            device_id=(lag_at(step), space),
            device_id_type=MESH,
        )
        copy.start()
        gather.append(copy)
    forward = []
    for step in range(lags):
        if step:
            gather[step - 1].wait_recv()
        spot = (space,) + place(lag_at(lags - step) if step else lag)
        for aside in range(1, spaces):
            copy = pltpu.make_async_remote_copy(
                src_ref=whole_ref.at[spot],
                dst_ref=whole_ref.at[spot],
                send_sem=send_3.at[step, aside],
                recv_sem=recv_3.at[step, aside],
                device_id=(lag, space_at(aside)),
                device_id_type=MESH,
            )
            copy.start()
            forward.append(copy)
    for copy in scatter + gather:
        copy.wait_send()
    for copy in small + forward:
        copy.wait()


def retire_kernel(lags, slot_ref, turned_ref, out_ref, landing, send_sem, recv_sem):
    lag, space = lax.axis_index("lag"), lax.axis_index("space")
    cycles, rows = out_ref.shape[0], out_ref.shape[1]

    def lag_at(step):
        return lax.rem(lag + step, lags)

    def place(block):
        return (slice(None), pl.ds(pl.multiple_of(block * rows, rows), rows))

    barrier = pltpu.get_barrier_semaphore()
    for step in range(1, lags):
        pl.semaphore_signal(barrier, inc=1, device_id=(lag_at(step), space), device_id_type=MESH)
    pl.semaphore_wait(barrier, lags - 1)
    copies = []
    for step in range(1, lags):
        copy = pltpu.make_async_remote_copy(
            src_ref=turned_ref.at[place(lag_at(step))],
            dst_ref=landing.at[step],
            send_sem=send_sem.at[step],
            recv_sem=recv_sem.at[step],
            device_id=(lag_at(step), space),
            device_id_type=MESH,
        )
        copy.start()
        copies.append(copy)
    mine = turned_ref[place(lag)]
    blocks = [mine[cycle] for cycle in range(cycles)]
    for step in range(1, lags):
        copies[step - 1].wait_recv()
        for cycle in range(cycles):
            target = slot_ref[(lags - 1 - cycle) % lags]
            blocks[cycle] = jnp.where(
                lag_at(lags - step) == target, landing[step, cycle], blocks[cycle]
            )
    for cycle in range(cycles):
        out_ref[cycle] = blocks[cycle]
    for copy in copies:
        copy.wait_send()


def dot(a, b):
    return jnp.dot(a, b, preferred_element_type=F32)


def parts_of(value, count):
    parts = []
    for _ in range(count):
        part = value.astype(BF16)
        parts.append(part)
        value = value - part.astype(F32)
    return parts


def dot_parts(value, right, count):
    total = None
    for part in parts_of(value, count):
        term = dot(part, right)
        total = term if total is None else total + term
    return total


def iota(shape, dim):
    return lax.broadcasted_iota(jnp.int32, shape, dim)


def column_of(row):
    n = row.shape[1]
    return jnp.sum(
        jnp.where(iota((n, n), 0) == iota((n, n), 1), row, 0.0), axis=1, keepdims=True
    )


def inverse_of(gram):
    n = gram.shape[0]
    at_row, at_column = iota((n, n), 0), iota((n, n), 1)
    for k in range(n):
        pivot = 1.0 / gram[k : k + 1, k : k + 1]
        column = gram[:, k : k + 1]
        rest = jnp.where(at_column == k, 0.0, gram)
        row = jnp.where(at_column[:1] == k, 1.0, gram[k : k + 1, :]) * pivot
        gram = jnp.where(at_row == k, row, rest - column * row)
    return gram


def analysis(values, spread, solved):
    centre = jnp.mean(values, axis=1, keepdims=True)
    anomaly = (values - centre).astype(BF16)
    cross = lax.dot_general(
        anomaly, spread, (((1,), (1,)), ((), ())), preferred_element_type=F32
    )
    return (values + dot_parts(cross, solved, 2)).astype(BF16)


def smoother_kernel(
    lags, slot_ref, slab_ref, whole_ref, shift_ref, coupling_ref, cells_ref, weight_ref,
    reading_ref, jitter_ref, variance_ref, out_ref, turned_ref, matrix, forecast,
):
    lag, space = lax.axis_index("lag"), lax.axis_index("space")
    spaces, own, members = whole_ref.shape
    total = spaces * own
    cycles = variance_ref.shape[0]
    corners = cells_ref.shape[2]
    source_cell = iota((total, own), 0)
    for part in range(spaces):
        cell = iota((total, own), 1) + part * own
        kept = jnp.zeros((1, own), F32)
        entry = jnp.zeros((total, own), F32)
        for k in range(shift_ref.shape[1]):
            weight = coupling_ref[part, k : k + 1, :]
            offset = shift_ref[part, k : k + 1, :]
            entry = entry + jnp.where(source_cell - cell == offset, weight, 0.0)
            kept = kept + weight
        entry = entry + jnp.where(source_cell == cell, 1.0 - kept, 0.0)
        matrix[:, part * own : (part + 1) * own] = entry
    power = FC_STEPS
    step = matrix[...]
    while power > 1:
        step = jnp.dot(step, step, precision=lax.Precision.HIGHEST, preferred_element_type=F32)
        power //= 2
    operator = parts_of(step.T, 2)

    state = slab_ref[...]
    newest = whole_ref[...].reshape(total, members)
    for cycle in range(cycles):
        target = slot_ref[(lags - 1 - cycle) % lags]
        ahead = (dot(operator[0], newest) + dot(operator[1], newest)).astype(BF16)
        measured, readings = [], []
        for part in range(spaces):
            wanted = cells_ref.shape[3]
            hold = jnp.zeros((own, wanted), F32)
            for q in range(corners):
                hold = hold + jnp.where(
                    iota((own, wanted), 0) == cells_ref[part, cycle, q : q + 1, :],
                    weight_ref[part, cycle, q : q + 1, :],
                    0.0,
                )
            measured.append(dot_parts(hold.T, ahead[part * own : (part + 1) * own], 3))
            readings.append(
                column_of(reading_ref[part, cycle : cycle + 1, :])
                + jnp.sqrt(
                    column_of(
                        variance_ref[cycle : cycle + 1, part * wanted : (part + 1) * wanted]
                    )
                )
                * jitter_ref[part, cycle]
            )
        measured = jnp.concatenate(measured, axis=0)
        readings = jnp.concatenate(readings, axis=0)
        spread = (measured - jnp.mean(measured, axis=1, keepdims=True)).astype(BF16)
        innovation = (readings - measured).astype(BF16)
        gram = lax.dot_general(
            spread, spread, (((1,), (1,)), ((), ())), preferred_element_type=F32
        )
        n = gram.shape[0]
        gram = gram + jnp.where(
            iota((n, n), 0) == iota((n, n), 1),
            (members - 1) * variance_ref[cycle : cycle + 1, :],
            0.0,
        )
        solved = dot_parts(inverse_of(gram), innovation, 3).astype(BF16)
        updated = analysis(state.astype(F32), spread, solved)
        fresh = analysis(ahead.astype(F32), spread, solved)
        turned_ref[cycle] = updated.astype(F32).T.astype(BF16)
        forecast[...] = fresh
        fresh_own = forecast[pl.ds(pl.multiple_of(space * own, own), own), :]
        state = jnp.where(lag == target, fresh_own, updated)
        newest = fresh
    out_ref[...] = state


def on_device(
    lags, spaces, ensemble, slot_order, neighbour_shift, edge_coupling, observation_cells,
    observation_weight, observation_reading, observation_variance, observation_jitter,
):
    slab = ensemble[0]
    cells, members = slab.shape
    cycles = observation_variance.shape[0]
    across = members // LANES
    rows = cells * across // lags
    smem = pl.BlockSpec(memory_space=pltpu.SMEM)
    vmem = pl.BlockSpec(memory_space=pltpu.VMEM)
    small = [
        neighbour_shift, edge_coupling, observation_cells, observation_weight,
        observation_reading, observation_jitter,
    ]
    dma = pltpu.SemaphoreType.DMA
    whole, *gathered = pl.pallas_call(
        functools.partial(exchange_kernel, lags, spaces),
        out_shape=[jax.ShapeDtypeStruct((spaces, cells, members), BF16)]
        + [jax.ShapeDtypeStruct((spaces,) + a.shape, a.dtype) for a in small],
        in_specs=[smem] + [vmem] * (1 + len(small)),
        out_specs=[vmem] * (1 + len(small)),
        scratch_shapes=[
            pltpu.VMEM((lags, rows, LANES), BF16),
            pltpu.VMEM((rows, LANES), BF16),
            dma((lags,)), dma((lags,)), dma((lags,)), dma((lags,)),
            dma((lags, spaces)), dma((lags, spaces)),
            dma((2, len(small), spaces)),
        ],
        compiler_params=pltpu.CompilerParams(
            collective_id=0, has_side_effects=True, vmem_limit_bytes=VMEM_BYTES
        ),
        name="exchange",
    )(slot_order, slab, *small)
    analysed, turned = pl.pallas_call(
        functools.partial(smoother_kernel, lags),
        out_shape=[
            jax.ShapeDtypeStruct((cells, members), BF16),
            jax.ShapeDtypeStruct((cycles, members, cells), BF16),
        ],
        in_specs=[smem] + [vmem] * 9,
        out_specs=[vmem] * 2,
        scratch_shapes=[
            pltpu.VMEM((spaces * cells, spaces * cells), F32),
            pltpu.VMEM((spaces * cells, members), BF16),
        ],
        compiler_params=pltpu.CompilerParams(vmem_limit_bytes=VMEM_BYTES),
        name="smoother",
    )(slot_order, slab, whole, *gathered, observation_variance)
    member_rows = members // lags
    retired = pl.pallas_call(
        functools.partial(retire_kernel, lags),
        out_shape=jax.ShapeDtypeStruct((cycles, member_rows, cells), BF16),
        in_specs=[smem, vmem],
        out_specs=vmem,
        scratch_shapes=[
            pltpu.VMEM((lags, cycles, member_rows, cells), BF16),
            dma((lags,)), dma((lags,)),
        ],
        compiler_params=pltpu.CompilerParams(
            collective_id=1, has_side_effects=True, vmem_limit_bytes=VMEM_BYTES
        ),
        name="retire",
    )(slot_order, turned)
    return analysed[None], retired


def solution(mesh):
    in_specs = (
        P("lag", "space", None),
        P(),
        P(None, "space"),
        P(None, "space"),
        P(None, None, "space"),
        P(None, None, "space"),
        P(None, "space"),
        P(),
        P(None, "space", None),
    )
    out_specs = (P("lag", "space", None), P(None, "lag", "space"))
    return jax.shard_map(
        functools.partial(on_device, mesh.shape["lag"], mesh.shape["space"]),
        mesh=mesh, in_specs=in_specs, out_specs=out_specs, check_vma=False,
    )
```

time: 497 us -> 59.3 us (0.12)
  the two profiles are of different devices: /device:TPU:1 before, /device:TPU:14 now
where the time goes in v1:
time: 59.3 us; the launch traced here: 59 us
  Pallas kernels  51.8 us (87%)
  local copies, waits for them, and re-layouts  6.57 us (11%)
  between operations  0.68 us (1%)
    pallas_call x1, Pallas kernels, on_device(): pl.pallas_call(functools.partial(retire_kernel, lags), out_shape=jax.Shap...  19.9 us
    pallas_call x1, Pallas kernels, on_device(): pl.pallas_call(functools.partial(exchange_kernel, lags, spaces), out_shap...  19.4 us
    pallas_call x1, Pallas kernels, on_device(): pl.pallas_call(functools.partial(smoother_kernel, lags), out_shape=[jax.S...  12.4 us
    unnamed x19, local copies, waits for them, and re-layouts  6.57 us

profile of v1, /device:TPU:14, one launch (start us, length us, event | category | flops | bytes accessed | tf_op | source)
XLA Modules:
  0.0 59.0 jit_solution(7330298682932184573)
XLA Ops:
  0.6 0.0 copy-start.2
  0.6 0.0 copy-start.7
  0.7 0.6 %copy-done.2 = s32[16]{0:T(128)S(1)} copy-done((s32[16]{0:T(128)S(1)}, s32[16]{0:T(128)}, u32[]{:S(2)}) %copy-start.2) | copy-done | bytes 88
  1.3 0.0 copy-done.7
  1.3 0.0 copy-start
  1.3 0.9 %copy-done = bf16[1,128,1024]{2,1,0:T(8,128)(2,1)S(1)} copy-done((bf16[1,128,1024]{2,1,0:T(8,128)(2,1)S(1)}, bf16[1,128,1024]{2,1,0:T(8,128)(2,1)}, u32[]{:S(2)}) %copy-start) | copy-done | bytes 262168
  2.3 0.0 copy-start.1
  2.3 0.9 %copy-done.1 = f32[2,16,1024]{2,1,0:T(8,128)S(1)} copy-done((f32[2,16,1024]{2,1,0:T(8,128)S(1)}, f32[2,16,1024]{2,1,0:T(8,128)}, u32[]{:S(2)}) %copy-start.1) | copy-done | bytes 131096
  3.2 0.0 copy-start.3
  3.2 0.7 %copy-done.3 = s32[6,128]{1,0:T(8,128)S(1)} copy-done((s32[6,128]{1,0:T(8,128)S(1)}, s32[6,128]{1,0:T(8,128)}, u32[]{:S(2)}) %copy-start.3) | copy-done | bytes 3096
  3.9 0.0 copy-start.4
  3.9 0.7 %copy-done.4 = f32[6,128]{1,0:T(8,128)S(1)} copy-done((f32[6,128]{1,0:T(8,128)S(1)}, f32[6,128]{1,0:T(8,128)}, u32[]{:S(2)}) %copy-start.4) | copy-done | bytes 3096
  4.6 0.0 copy-start.5
  4.6 0.7 %copy-done.5 = s32[2,4,16]{2,1,0:T(4,128)S(1)} copy-done((s32[2,4,16]{2,1,0:T(4,128)S(1)}, s32[2,4,16]{2,1,0:T(4,128)}, u32[]{:S(2)}) %copy-start.5) | copy-done | bytes 536
  5.2 0.0 copy-start.6
  5.2 0.7 %copy-done.6 = f32[2,4,16]{2,1,0:T(4,128)S(1)} copy-done((f32[2,4,16]{2,1,0:T(4,128)S(1)}, f32[2,4,16]{2,1,0:T(4,128)}, u32[]{:S(2)}) %copy-start.6) | copy-done | bytes 536
  5.9 19.4 %exchange.1 = (bf16[2,128,1024]{2,1,0:T(8,128)(2,1)S(1)}, s32[2,6,128]{2,1,0:T(8,128)S(1)}, f32[2,6,128]{2,1,0:T(8,128)S(1)}, s32[2,2,4,16]{3,2,1,0:T(4,128)S(1)...) custom-call(s32[16]{0:T(128)S(1)} %copy-done.2, ...), custom_call_target="tpu_custom_call" | custom-call | tf_op jit(solution)/shard_map/exchange/pallas_call | solution.py:303
  25.4 0.0 copy-start.8
  25.4 0.7 %copy-done.8 = f32[2,32]{1,0:T(2,128)S(1)} copy-done((f32[2,32]{1,0:T(2,128)S(1)}, f32[2,32]{1,0:T(2,128)}, u32[]{:S(2)}) %copy-start.8) | copy-done | bytes 280
  26.1 12.4 %smoother.1 = (bf16[128,1024]{1,0:T(8,128)(2,1)}, bf16[2,1024,128]{2,1,0:T(8,128)(2,1)S(1)}) custom-call(s32[16]{0:T(128)S(1)} %copy-done.2, bf16[128,1024]{1,0:T(8,128)(2,1)S(1)} %bitcast.3, bf16[2,128,1024]{2,1,0:T(8,128)(2,1)S(1)} %get-tuple-element.11.whole_ref, s32[2,6,128]{2,1,0:T(8,128)S(1)} %get-tuple-element.12.shift_ref, ...), custom_call_target="tpu_custom_call" | custom-call | tf_op jit(solution)/shard_map/smoother/pallas_call | solution.py:321
  38.5 19.9 %retire.1 = bf16[2,64,128]{2,1,0:T(8,128)(2,1)S(1)} custom-call(s32[16]{0:T(128)S(1)} %copy-done.2, bf16[2,1024,128]{2,1,0:T(8,128)(2,1)S(1)} %get-tuple-element.19.turned_ref), custom_call_target="tpu_custom_call" | custom-call | tf_op jit(solution)/shard_map/retire/pallas_call | solution.py:337
  58.4 0.6 %copy.12 = bf16[2,64,128]{2,1,0:T(8,128)(2,1)} copy(bf16[2,64,128]{2,1,0:T(8,128)(2,1)S(1)} %retire.1) | data formatting | bytes 65536
Async XLA Ops:
  0.6 0.7 %copy-start.2 = (s32[16]{0:T(128)S(1)}, s32[16]{0:T(128)}, u32[]{:S(2)}) copy-start(s32[16]{0:T(128)} %slot_ref.5) | copy-start | bytes 196
  0.6 0.7 %copy-start.7 = (f32[2,16]{1,0:T(2,128)S(1)}, f32[2,16]{1,0:T(2,128)}, u32[]{:S(2)}) copy-start(f32[2,16]{1,0:T(2,128)} %refs_4_.1) | copy-start | bytes 388
  1.3 0.9 %copy-start = (bf16[1,128,1024]{2,1,0:T(8,128)(2,1)S(1)}, bf16[1,128,1024]{2,1,0:T(8,128)(2,1)}, u32[]{:S(2)}) copy-start(bf16[1,128,1024]{2,1,0:T(8,128)(2,1)} %param.9) | copy-start | bytes 786436
  2.3 0.9 %copy-start.1 = (f32[2,16,1024]{2,1,0:T(8,128)S(1)}, f32[2,16,1024]{2,1,0:T(8,128)}, u32[]{:S(2)}) copy-start(f32[2,16,1024]{2,1,0:T(8,128)} %refs_5_.1) | copy-start | bytes 393220
  3.2 0.7 %copy-start.3 = (s32[6,128]{1,0:T(8,128)S(1)}, s32[6,128]{1,0:T(8,128)}, u32[]{:S(2)}) copy-start(s32[6,128]{1,0:T(8,128)} %refs_0_.1) | copy-start | bytes 9220
  3.9 0.7 %copy-start.4 = (f32[6,128]{1,0:T(8,128)S(1)}, f32[6,128]{1,0:T(8,128)}, u32[]{:S(2)}) copy-start(f32[6,128]{1,0:T(8,128)} %refs_1_.1) | copy-start | bytes 9220
  4.6 0.7 %copy-start.5 = (s32[2,4,16]{2,1,0:T(4,128)S(1)}, s32[2,4,16]{2,1,0:T(4,128)}, u32[]{:S(2)}) copy-start(s32[2,4,16]{2,1,0:T(4,128)} %refs_2_.1) | copy-start | bytes 1540
  5.2 0.7 %copy-start.6 = (f32[2,4,16]{2,1,0:T(4,128)S(1)}, f32[2,4,16]{2,1,0:T(4,128)}, u32[]{:S(2)}) copy-start(f32[2,4,16]{2,1,0:T(4,128)} %refs_3_.1) | copy-start | bytes 1540
  25.4 0.7 %copy-start.8 = (f32[2,32]{1,0:T(2,128)S(1)}, f32[2,32]{1,0:T(2,128)}, u32[]{:S(2)}) copy-start(f32[2,32]{1,0:T(2,128)} %variance_ref.1) | copy-start | bytes 772

commit v2 on v0

v2 whole, which is shorter than its diff:
```python
import functools
import jax
import jax.numpy as jnp
from jax import lax
from jax.experimental import pallas as pl
from jax.experimental.pallas import tpu as pltpu
from jax.sharding import PartitionSpec as P

FC_STEPS = 4
LANES = 128
MESH = pl.DeviceIdType.MESH
VMEM_BYTES = 50 * 1024 * 1024
F32 = jnp.float32
BF16 = jnp.bfloat16


def dot(a, b):
    return jnp.dot(a, b, preferred_element_type=F32)


def parts_of(value, count):
    parts = []
    for _ in range(count):
        part = value.astype(BF16)
        parts.append(part)
        value = value - part.astype(F32)
    return parts


def dot_parts(value, right, count):
    total = None
    for part in parts_of(value, count):
        term = dot(part, right)
        total = term if total is None else total + term
    return total


def iota(shape, dim):
    return lax.broadcasted_iota(jnp.int32, shape, dim)


def column_of(row):
    n = row.shape[1]
    return jnp.sum(
        jnp.where(iota((n, n), 0) == iota((n, n), 1), row, 0.0), axis=1, keepdims=True
    )


def inverse_of(gram):
    n = gram.shape[0]
    at_row, at_column = iota((n, n), 0), iota((n, n), 1)
    for k in range(n):
        pivot = 1.0 / gram[k : k + 1, k : k + 1]
        column = gram[:, k : k + 1]
        rest = jnp.where(at_column == k, 0.0, gram)
        row = jnp.where(at_column[:1] == k, 1.0, gram[k : k + 1, :]) * pivot
        gram = jnp.where(at_row == k, row, rest - column * row)
    return gram


def anomaly_of(values):
    centre = jnp.mean(values, axis=1, keepdims=True)
    return (values - centre).astype(BF16)


def across_members(a, b):
    return lax.dot_general(a, b, (((1,), (1,)), ((), ())), preferred_element_type=F32)


def smoother_kernel(lags, spaces, slot_ref, slab_hbm, variance_ref, *refs):
    small_in, refs = refs[:6], refs[6:]
    out_ref, retired_ref, slab_ref, whole_ref, refs = refs[0], refs[1], refs[2], refs[3], refs[4:]
    small_all, refs = refs[:6], refs[6:]
    (
        matrix, forecast, anomaly, turned, cross_out, solved_turned, landing, chosen,
        landing_turned, landing_cross, local_sem, send_l, recv_l, send_3, recv_3, send_s, recv_s,
    ) = refs
    shift_ref, coupling_ref, cells_ref, weight_ref, reading_ref, jitter_ref = small_all
    lag, space = lax.axis_index("lag"), lax.axis_index("space")
    own, members = slab_ref.shape
    total = spaces * own
    cycles = variance_ref.shape[0]
    corners, wanted = cells_ref.shape[2], cells_ref.shape[3]
    across = members // LANES
    rows = own * across // lags
    member_rows = members // lags

    def place(block):
        return (
            pl.ds(pl.multiple_of((block // across) * rows, rows), rows),
            pl.ds(pl.multiple_of((block % across) * LANES, LANES), LANES),
        )

    def member_place(block):
        return (pl.ds(pl.multiple_of(block * member_rows, member_rows), member_rows),)

    def lag_at(step):
        return lax.rem(lag + step, lags)

    def space_at(step):
        return lax.rem(space + step, spaces)

    def send_lag(kind, step, source, target):
        copy = pltpu.make_async_remote_copy(
            src_ref=source,
            dst_ref=target,
            send_sem=send_l.at[kind, step],
            recv_sem=recv_l.at[kind, step],
            device_id=(lag_at(step), space),
            device_id_type=MESH,
        )
        copy.start()
        return copy

    local = [pltpu.make_async_copy(slab_hbm, slab_ref, local_sem.at[6])]
    for item in range(6):
        local.append(
            pltpu.make_async_copy(small_in[item], small_all[item].at[space], local_sem.at[item])
        )
    for copy in local:
        copy.start()
    barrier = pltpu.get_barrier_semaphore()
    for step in range(1, lags):
        pl.semaphore_signal(barrier, inc=1, device_id=(lag_at(step), space), device_id_type=MESH)
    for step in range(1, spaces):
        pl.semaphore_signal(barrier, inc=1, device_id=(lag, space_at(step)), device_id_type=MESH)
    pl.semaphore_wait(barrier, lags - 1 + spaces - 1)

    scatter = [
        send_lag(0, step, slab_hbm.at[place(lag_at(step))], landing.at[step])
        for step in range(1, lags)
    ]
    small = []
    for step in range(1, spaces):
        for item in range(6):
            copy = pltpu.make_async_remote_copy(
                src_ref=small_in[item],
                dst_ref=small_all[item].at[space],
                send_sem=send_s.at[item, step],
                recv_sem=recv_s.at[item, step],
                device_id=(lag, space_at(step)),
                device_id_type=MESH,
            )
            copy.start()
            small.append(copy)
    for copy in local:
        copy.wait()
    for copy in small:
        copy.wait()

    source_cell = iota((total, own), 0)
    for part in range(spaces):
        cell = iota((total, own), 1) + part * own
        kept = jnp.zeros((1, own), F32)
        entry = jnp.zeros((total, own), F32)
        for k in range(shift_ref.shape[1]):
            weight = coupling_ref[part, k : k + 1, :]
            offset = shift_ref[part, k : k + 1, :]
            entry = entry + jnp.where(source_cell - cell == offset, weight, 0.0)
            kept = kept + weight
        entry = entry + jnp.where(source_cell == cell, 1.0 - kept, 0.0)
        matrix[:, part * own : (part + 1) * own] = entry
    power = FC_STEPS
    one = matrix[...]
    while power > 1:
        one = jnp.dot(one, one, precision=lax.Precision.HIGHEST, preferred_element_type=F32)
        power //= 2
    operator = parts_of(one.T, 2)
    holds, readings = [], []
    for cycle in range(cycles):
        hold_cycle, reading_cycle = [], []
        for part in range(spaces):
            hold = jnp.zeros((own, wanted), F32)
            for q in range(corners):
                hold = hold + jnp.where(
                    iota((own, wanted), 0) == cells_ref[part, cycle, q : q + 1, :],
                    weight_ref[part, cycle, q : q + 1, :],
                    0.0,
                )
            hold_cycle.append(hold.T)
            variance = variance_ref[cycle : cycle + 1, part * wanted : (part + 1) * wanted]
            reading_cycle.append(
                column_of(reading_ref[part, cycle : cycle + 1, :])
                + jnp.sqrt(column_of(variance)) * jitter_ref[part, cycle]
            )
        holds.append(hold_cycle)
        readings.append(jnp.concatenate(reading_cycle, axis=0))

    source = slot_ref[0]
    block = jnp.where(lag == source, slab_ref[place(lag)], jnp.zeros((rows, LANES), BF16))
    for step in range(1, lags):
        scatter[step - 1].wait_recv()
        block = jnp.where(lag_at(lags - step) == source, landing[step], block)
    chosen[...] = block
    whole_ref[(space,) + place(lag)] = block
    gather = [
        send_lag(1, step, chosen, whole_ref.at[(space,) + place(lag)]) for step in range(1, lags)
    ]
    anomaly[...] = anomaly_of(slab_ref[...].astype(F32))
    forward = []
    for step in range(lags):
        if step:
            gather[step - 1].wait_recv()
        spot = (space,) + place(lag_at(lags - step) if step else lag)
        for aside in range(1, spaces):
            copy = pltpu.make_async_remote_copy(
                src_ref=whole_ref.at[spot],
                dst_ref=whole_ref.at[spot],
                send_sem=send_3.at[step, aside],
                recv_sem=recv_3.at[step, aside],
                device_id=(lag, space_at(aside)),
                device_id_type=MESH,
            )
            copy.start()
            forward.append(copy)
    for copy in forward:
        copy.wait_recv()

    def observed(cycle, ahead):
        measured = jnp.concatenate(
            [
                dot_parts(holds[cycle][part], ahead[part * own : (part + 1) * own], 3)
                for part in range(spaces)
            ],
            axis=0,
        )
        return anomaly_of(measured), (readings[cycle] - measured).astype(BF16)

    def solve(cycle, spread, innovation):
        gram = across_members(spread, spread)
        n = gram.shape[0]
        gram = gram + jnp.where(
            iota((n, n), 0) == iota((n, n), 1),
            (members - 1) * variance_ref[cycle : cycle + 1, :],
            0.0,
        )
        return dot_parts(inverse_of(gram), innovation, 3).astype(BF16)

    def own_rows(value):
        forecast[...] = value
        return forecast[pl.ds(pl.multiple_of(space * own, own), own), :]

    target_0, target_1 = slot_ref[lags - 1], slot_ref[lags - 2]

    newest = whole_ref[...].reshape(total, members)
    ahead = (dot(operator[0], newest) + dot(operator[1], newest)).astype(BF16)
    spread, innovation = observed(0, ahead)
    cross = across_members(anomaly[...], spread)
    ahead_f = ahead.astype(F32)
    cross_ahead = across_members(anomaly_of(ahead_f), spread)
    solved = solve(0, spread, innovation)
    updated = slab_ref[...].astype(F32) + dot_parts(cross, solved, 2)
    turned[...] = updated.T.astype(BF16)
    exchanged = [
        send_lag(2, step, turned.at[member_place(lag_at(step))], landing_turned.at[step])
        for step in range(1, lags)
    ]
    newest = (ahead_f + dot_parts(cross_ahead, solved, 2)).astype(BF16)
    state = jnp.where(lag == target_0, own_rows(newest), updated.astype(BF16)).astype(F32)

    ahead = (dot(operator[0], newest) + dot(operator[1], newest)).astype(BF16)
    spread, innovation = observed(1, ahead)
    cross = across_members(anomaly_of(state), spread)
    cross_out[...] = cross.T.astype(BF16)
    crosses = [
        send_lag(3, step, cross_out, landing_cross.at[step]) for step in range(1, lags)
    ]
    ahead_own = own_rows(ahead).astype(F32)
    cross_ahead = across_members(anomaly_of(ahead_own), spread)
    solved = solve(1, spread, innovation)
    base = jnp.where(lag == target_1, ahead_own, state)
    cross = jnp.where(lag == target_1, cross_ahead, cross)
    out_ref[...] = (base + dot_parts(cross, solved, 2)).astype(BF16)
    solved_turned[...] = solved.astype(F32).T

    first = turned[member_place(lag)]
    second = first
    for step in range(1, lags):
        exchanged[step - 1].wait_recv()
        sender = lag_at(lags - step)
        first = jnp.where(sender == target_0, landing_turned[step], first)
        second = jnp.where(sender == target_1, landing_turned[step], second)
    retired_ref[0] = first
    cross_turned = cross_out[...]
    for step in range(1, lags):
        crosses[step - 1].wait_recv()
        sender = lag_at(lags - step)
        cross_turned = jnp.where(sender == target_1, landing_cross[step], cross_turned)
    mine = solved_turned[member_place(lag)].astype(BF16)
    retired_ref[1] = (second.astype(F32) + dot(mine, cross_turned)).astype(BF16)
    for copy in scatter + gather + forward + exchanged + crosses:
        copy.wait_send()


def on_device(
    lags, spaces, ensemble, slot_order, neighbour_shift, edge_coupling, observation_cells,
    observation_weight, observation_reading, observation_variance, observation_jitter,
):
    slab = ensemble[0]
    own, members = slab.shape
    cycles, count = observation_variance.shape
    rows = own * (members // LANES) // lags
    member_rows = members // lags
    total = spaces * own
    smem = pl.BlockSpec(memory_space=pltpu.SMEM)
    vmem = pl.BlockSpec(memory_space=pltpu.VMEM)
    hbm = pl.BlockSpec(memory_space=pltpu.HBM)
    small = [
        neighbour_shift, edge_coupling, observation_cells, observation_weight,
        observation_reading, observation_jitter,
    ]
    dma = pltpu.SemaphoreType.DMA
    analysed, retired = pl.pallas_call(
        functools.partial(smoother_kernel, lags, spaces),
        out_shape=[
            jax.ShapeDtypeStruct((own, members), BF16),
            jax.ShapeDtypeStruct((cycles, member_rows, own), BF16),
        ],
        in_specs=[smem, hbm, vmem] + [hbm] * len(small),
        out_specs=[vmem] * 2,
        scratch_shapes=[
            pltpu.VMEM((own, members), BF16),
            pltpu.VMEM((spaces, own, members), BF16),
        ]
        + [pltpu.VMEM((spaces,) + a.shape, a.dtype) for a in small]
        + [
            pltpu.VMEM((total, total), F32),
            pltpu.VMEM((total, members), BF16),
            pltpu.VMEM((own, members), BF16),
            pltpu.VMEM((members, own), BF16),
            pltpu.VMEM((count, own), BF16),
            pltpu.VMEM((members, count), F32),
            pltpu.VMEM((lags, rows, LANES), BF16),
            pltpu.VMEM((rows, LANES), BF16),
            pltpu.VMEM((lags, member_rows, own), BF16),
            pltpu.VMEM((lags, count, own), BF16),
            dma((7,)),
            dma((4, lags)), dma((4, lags)),
            dma((lags, spaces)), dma((lags, spaces)),
            dma((6, spaces)), dma((6, spaces)),
        ],
        compiler_params=pltpu.CompilerParams(
            collective_id=0, has_side_effects=True, vmem_limit_bytes=VMEM_BYTES
        ),
        name="smoother",
    )(slot_order, slab, observation_variance, *small)
    return analysed[None], retired


def solution(mesh):
    in_specs = (
        P("lag", "space", None),
        P(),
        P(None, "space"),
        P(None, "space"),
        P(None, None, "space"),
        P(None, None, "space"),
        P(None, "space"),
        P(),
        P(None, "space", None),
    )
    out_specs = (P("lag", "space", None), P(None, "lag", "space"))
    return jax.shard_map(
        functools.partial(on_device, mesh.shape["lag"], mesh.shape["space"]),
        mesh=mesh, in_specs=in_specs, out_specs=out_specs, check_vma=False,
    )
```

time: 497 us -> 46.7 us (0.09)
  waiting for transfers between devices: 317 us -> 0 us
  local copies, waits for them, and re-layouts: 72.2 us -> 7.26 us
  other arithmetic: 38.9 us -> 0 us
  Pallas kernels: 0 us -> 38.4 us
  starting transfers between devices: 33.4 us -> 0 us
  between operations: 16.7 us -> 0.67 us
  matrix products: 7.82 us -> 0 us
  blocking collectives: 7.55 us -> 0 us
    psum x3 -> x0, waiting for transfers between devices: 307 us -> none  [spread_2(): return lax.psum(kept, axis)]
    gather x56 -> x0, local copies, waits for them, and re-layouts: 61.5 us -> none  [the longest x48 56.3 us: relax_once(): padded[picked] - centre]
    pallas_call x0 -> x1, Pallas kernels: none -> 38.4 us  [on_device(): pl.pallas_call(functools.partial(smoother_kernel, lags, spaces), out_shap...]
    ppermute x16 -> x0, starting transfers between devices: 33.3 us -> none  [the longest x8 22.7 us: padded_2(): lax.ppermute(head, axis, [((i + 1) % count, i) for i in range(ends)])]
    another operation x11 -> x0, other arithmetic: 13.4 us -> none  [the longest x6 7.2 us: solve_weights(): factor = jnp.linalg.cholesky(gram_matrix)]
    add x6 -> x0, other arithmetic: 9.84 us -> none  [relax_once(): return centre + accrued]
    ppermute x16 -> x0, waiting for transfers between devices: 9.26 us -> none  [the longest x8 9.24 us: padded_2(): lax.ppermute(tail, axis, [(i, (i + 1) % count) for i in range(ends)])]
    all_gather x4 -> x0, blocking collectives: 7.55 us -> none  [the longest x2 3.86 us: solve_weights(): lax.all_gather(innovation, 'space', axis=0, tiled=True)]
  transfers between devices with their start and end apart: 19 -> 0, of which waited for: 11 -> 0; matrix products, arithmetic and copies ran while one was open for 3% -> 0% of each run, Pallas kernels for 0% -> 0%
where the time goes in v2:
time: 46.7 us; the launch traced here: 46.4 us
  Pallas kernels  38.4 us (82%)
  local copies, waits for them, and re-layouts  7.26 us (16%)
  between operations  0.67 us (1%)
    pallas_call x1, Pallas kernels, on_device(): pl.pallas_call(functools.partial(smoother_kernel, lags, spaces), out_shap...  38.4 us
    unnamed x20, local copies, waits for them, and re-layouts  7.26 us

profile of v2, /device:TPU:1, one launch (start us, length us, event | category | flops | bytes accessed | tf_op | source)
XLA Modules:
  0.0 46.4 jit_solution(18290635684636445429)
XLA Ops:
  0.6 0.0 copy-start.6
  0.6 0.0 copy-start.8
  0.7 0.7 %copy-done.6 = f32[2,32]{1,0:T(2,128)S(1)} copy-done((f32[2,32]{1,0:T(2,128)S(1)}, f32[2,32]{1,0:T(2,128)}, u32[]{:S(2)}) %copy-start.6) | copy-done | bytes 280
  1.3 0.0 copy-done.8
  1.3 0.0 copy-start
  1.3 0.9 %copy-done = bf16[1,128,1024]{2,1,0:T(8,128)(2,1)S(1)} copy-done((bf16[1,128,1024]{2,1,0:T(8,128)(2,1)S(1)}, bf16[1,128,1024]{2,1,0:T(8,128)(2,1)}, u32[]{:S(2)}) %copy-start) | copy-done | bytes 262168
  2.3 0.0 copy-start.1
  2.3 0.9 %copy-done.1 = f32[2,16,1024]{2,1,0:T(8,128)S(1)} copy-done((f32[2,16,1024]{2,1,0:T(8,128)S(1)}, f32[2,16,1024]{2,1,0:T(8,128)}, u32[]{:S(2)}) %copy-start.1) | copy-done | bytes 131096
  3.2 0.0 copy-start.2
  3.2 0.7 %copy-done.2 = s32[6,128]{1,0:T(8,128)S(1)} copy-done((s32[6,128]{1,0:T(8,128)S(1)}, s32[6,128]{1,0:T(8,128)}, u32[]{:S(2)}) %copy-start.2) | copy-done | bytes 3096
  3.9 0.0 copy-start.3
  3.9 0.7 %copy-done.3 = f32[6,128]{1,0:T(8,128)S(1)} copy-done((f32[6,128]{1,0:T(8,128)S(1)}, f32[6,128]{1,0:T(8,128)}, u32[]{:S(2)}) %copy-start.3) | copy-done | bytes 3096
  4.5 0.0 copy-start.4
  4.5 0.7 %copy-done.4 = s32[2,4,16]{2,1,0:T(4,128)S(1)} copy-done((s32[2,4,16]{2,1,0:T(4,128)S(1)}, s32[2,4,16]{2,1,0:T(4,128)}, u32[]{:S(2)}) %copy-start.4) | copy-done | bytes 536
  5.2 0.0 copy-start.5
  5.2 0.7 %copy-done.5 = f32[2,4,16]{2,1,0:T(4,128)S(1)} copy-done((f32[2,4,16]{2,1,0:T(4,128)S(1)}, f32[2,4,16]{2,1,0:T(4,128)}, u32[]{:S(2)}) %copy-start.5) | copy-done | bytes 536
  5.9 0.0 copy-start.7
  5.9 0.7 %copy-done.7 = f32[2,16]{1,0:T(2,128)S(1)} copy-done((f32[2,16]{1,0:T(2,128)S(1)}, f32[2,16]{1,0:T(2,128)}, u32[]{:S(2)}) %copy-start.7) | copy-done | bytes 152
  6.6 38.4 %smoother.1 = (bf16[128,1024]{1,0:T(8,128)(2,1)S(1)}, bf16[2,64,128]{2,1,0:T(8,128)(2,1)S(1)}) custom-call(s32[16]{0:T(128)S(1)} %copy-done.8, bf16[128,1024]{1,0:T(8,128)(2,1)S(1)} %bitcast.2, f32[2,32]{1,0:T(2,128)S(1)} %copy-done.6, s32[6,128]{1,0:T(8,128)S(1)} %copy-done.2, f32[6,128]{1,0:T(8,128)S(1)} %copy-done.3, s32[2,4,16]{2,1,0:T(4,128)S(1)} %copy-done.4, ...), custom_call_target="tpu_custom_call" | custom-call | tf_op jit(solution)/shard_map/smoother/pallas_call | solution.py:313
  45.1 0.7 %copy.13 = bf16[1,128,1024]{2,1,0:T(8,128)(2,1)} copy(bf16[1,128,1024]{2,1,0:T(8,128)(2,1)S(1)} %bitcast.3) | data formatting | bytes 524288
  45.8 0.6 %copy.14 = bf16[2,64,128]{2,1,0:T(8,128)(2,1)} copy(bf16[2,64,128]{2,1,0:T(8,128)(2,1)S(1)} %get-tuple-element.9) | data formatting | bytes 65536
Async XLA Ops:
  0.6 0.7 %copy-start.6 = (f32[2,32]{1,0:T(2,128)S(1)}, f32[2,32]{1,0:T(2,128)}, u32[]{:S(2)}) copy-start(f32[2,32]{1,0:T(2,128)} %variance_ref.1) | copy-start | bytes 772
  0.6 0.7 %copy-start.8 = (s32[16]{0:T(128)S(1)}, s32[16]{0:T(128)}, u32[]{:S(2)}) copy-start(s32[16]{0:T(128)} %slot_ref.1) | copy-start | bytes 196
  1.3 1.0 %copy-start = (bf16[1,128,1024]{2,1,0:T(8,128)(2,1)S(1)}, bf16[1,128,1024]{2,1,0:T(8,128)(2,1)}, u32[]{:S(2)}) copy-start(bf16[1,128,1024]{2,1,0:T(8,128)(2,1)} %param.9) | copy-start | bytes 786436
  2.3 0.9 %copy-start.1 = (f32[2,16,1024]{2,1,0:T(8,128)S(1)}, f32[2,16,1024]{2,1,0:T(8,128)}, u32[]{:S(2)}) copy-start(f32[2,16,1024]{2,1,0:T(8,128)} %refs_5_.1) | copy-start | bytes 393220
  3.2 0.7 %copy-start.2 = (s32[6,128]{1,0:T(8,128)S(1)}, s32[6,128]{1,0:T(8,128)}, u32[]{:S(2)}) copy-start(s32[6,128]{1,0:T(8,128)} %refs_0_.1) | copy-start | bytes 9220
  3.9 0.7 %copy-start.3 = (f32[6,128]{1,0:T(8,128)S(1)}, f32[6,128]{1,0:T(8,128)}, u32[]{:S(2)}) copy-start(f32[6,128]{1,0:T(8,128)} %refs_1_.1) | copy-start | bytes 9220
  4.5 0.7 %copy-start.4 = (s32[2,4,16]{2,1,0:T(4,128)S(1)}, s32[2,4,16]{2,1,0:T(4,128)}, u32[]{:S(2)}) copy-start(s32[2,4,16]{2,1,0:T(4,128)} %refs_2_.1) | copy-start | bytes 1540
  5.2 0.7 %copy-start.5 = (f32[2,4,16]{2,1,0:T(4,128)S(1)}, f32[2,4,16]{2,1,0:T(4,128)}, u32[]{:S(2)}) copy-start(f32[2,4,16]{2,1,0:T(4,128)} %refs_3_.1) | copy-start | bytes 1540
  5.9 0.7 %copy-start.7 = (f32[2,16]{1,0:T(2,128)S(1)}, f32[2,16]{1,0:T(2,128)}, u32[]{:S(2)}) copy-start(f32[2,16]{1,0:T(2,128)} %refs_4_.1) | copy-start | bytes 388

commit v3 on v2

--- a/solution.py
+++ b/solution.py
@@ -9,7 +9,7 @@
 FC_STEPS = 4
 LANES = 128
 MESH = pl.DeviceIdType.MESH
-VMEM_BYTES = 50 * 1024 * 1024
+VMEM_BYTES = 64 * 1024 * 1024
 F32 = jnp.float32
 BF16 = jnp.bfloat16
 
@@ -49,12 +49,20 @@
 def inverse_of(gram):
     n = gram.shape[0]
     at_row, at_column = iota((n, n), 0), iota((n, n), 1)
-    for k in range(n):
-        pivot = 1.0 / gram[k : k + 1, k : k + 1]
-        column = gram[:, k : k + 1]
-        rest = jnp.where(at_column == k, 0.0, gram)
-        row = jnp.where(at_column[:1] == k, 1.0, gram[k : k + 1, :]) * pivot
-        gram = jnp.where(at_row == k, row, rest - column * row)
+    line = at_column[:1]
+    for k in range(0, n, 2):
+        left = jnp.broadcast_to(gram[:, k : k + 1], (n, n))
+        right = jnp.broadcast_to(gram[:, k + 1 : k + 2], (n, n))
+        a, b, d = left[k : k + 1], left[k + 1 : k + 2], right[k + 1 : k + 2]
+        scale = 1.0 / (a * d - b * b)
+        pivots = (line == k) | (line == k + 1)
+        upper = jnp.where(pivots, jnp.where(line == k, 1.0, 0.0), gram[k : k + 1])
+        lower = jnp.where(pivots, jnp.where(line == k, 0.0, 1.0), gram[k + 1 : k + 2])
+        first = (d * upper - b * lower) * scale
+        second = (a * lower - b * upper) * scale
+        rest = jnp.where((at_column == k) | (at_column == k + 1), 0.0, gram)
+        rest = rest - left * first - right * second
+        gram = jnp.where(at_row == k, first, jnp.where(at_row == k + 1, second, rest))
     return gram
 
 
@@ -67,12 +75,12 @@
     return lax.dot_general(a, b, (((1,), (1,)), ((), ())), preferred_element_type=F32)
 
 
-def smoother_kernel(lags, spaces, slot_ref, slab_hbm, variance_ref, *refs):
+def smoother_kernel(lags, spaces, slot_ref, slab_hbm, variance_hbm, *refs):
     small_in, refs = refs[:6], refs[6:]
     out_ref, retired_ref, slab_ref, whole_ref, refs = refs[0], refs[1], refs[2], refs[3], refs[4:]
     small_all, refs = refs[:6], refs[6:]
     (
-        matrix, forecast, anomaly, turned, cross_out, solved_turned, landing, chosen,
+        variance_ref, matrix, forecast, anomaly, turned, cross_out, solved_turned, landing, chosen,
         landing_turned, landing_cross, local_sem, send_l, recv_l, send_3, recv_3, send_s, recv_s,
     ) = refs
     shift_ref, coupling_ref, cells_ref, weight_ref, reading_ref, jitter_ref = small_all
@@ -112,7 +120,10 @@
         copy.start()
         return copy
 
-    local = [pltpu.make_async_copy(slab_hbm, slab_ref, local_sem.at[6])]
+    local = [
+        pltpu.make_async_copy(slab_hbm, slab_ref, local_sem.at[6]),
+        pltpu.make_async_copy(variance_hbm, variance_ref, local_sem.at[7]),
+    ]
     for item in range(6):
         local.append(
             pltpu.make_async_copy(small_in[item], small_all[item].at[space], local_sem.at[item])
@@ -316,7 +327,7 @@
             jax.ShapeDtypeStruct((own, members), BF16),
             jax.ShapeDtypeStruct((cycles, member_rows, own), BF16),
         ],
-        in_specs=[smem, hbm, vmem] + [hbm] * len(small),
+        in_specs=[smem, hbm, hbm] + [hbm] * len(small),
         out_specs=[vmem] * 2,
         scratch_shapes=[
             pltpu.VMEM((own, members), BF16),
@@ -324,6 +335,7 @@
         ]
         + [pltpu.VMEM((spaces,) + a.shape, a.dtype) for a in small]
         + [
+            pltpu.VMEM((cycles, count), F32),
             pltpu.VMEM((total, total), F32),
             pltpu.VMEM((total, members), BF16),
             pltpu.VMEM((own, members), BF16),
@@ -334,7 +346,7 @@
             pltpu.VMEM((rows, LANES), BF16),
             pltpu.VMEM((lags, member_rows, own), BF16),
             pltpu.VMEM((lags, count, own), BF16),
-            dma((7,)),
+            dma((8,)),
             dma((4, lags)), dma((4, lags)),
             dma((lags, spaces)), dma((lags, spaces)),
             dma((6, spaces)), dma((6, spaces)),

time: 46.7 us -> 41.3 us (0.88)
  local copies, waits for them, and re-layouts: 7.26 us -> 2.29 us
    unnamed x20 -> x4, local copies, waits for them, and re-layouts: 7.26 us -> 2.29 us
where the time goes in v3:
time: 41.3 us; the launch traced here: 41.1 us
  Pallas kernels  38.2 us (92%)
  local copies, waits for them, and re-layouts  2.29 us (6%)
  between operations  0.65 us (2%)
    pallas_call x1, Pallas kernels, on_device(): pl.pallas_call(functools.partial(smoother_kernel, lags, spaces), out_shap...  38.2 us
    unnamed x4, local copies, waits for them, and re-layouts  2.29 us

profile of v3, /device:TPU:1, one launch (start us, length us, event | category | flops | bytes accessed | tf_op | source)
XLA Modules:
  0.0 41.1 jit_solution(6785877442859814838)
XLA Ops:
  0.6 38.2 %smoother.1 = (bf16[128,1024]{1,0:T(8,128)(2,1)}, bf16[2,64,128]{2,1,0:T(8,128)(2,1)}) custom-call(s32[16]{0:T(128)} %slot_ref.1, bf16[128,1024]{1,0:T(8,128)(2,1)} %bitcast.2, f32[2,32]{1,0:T(2,128)} %variance_hbm.1, s32[6,128]{1,0:T(8,128)} %refs_0_.1, f32[6,128]{1,0:T(8,128)} %refs_1_.1, s32[2,4,16]{2,1,0:T(4,128)} %refs_2_.1, f32[2,4,16]{2,1,0:T(4,128)} %refs_3_.1, ...), custom_call_target="tpu_custom_call" | custom-call | tf_op jit(solution)/shard_map/smoother/pallas_call | solution.py:324
  38.8 0.0 copy-start
  38.8 1.7 %copy.13 = bf16[1,128,1024]{2,1,0:T(8,128)(2,1)} copy(bf16[1,128,1024]{2,1,0:T(8,128)(2,1)} %bitcast.3) | data formatting | bytes 524288
  40.5 0.0 copy-done
  40.5 0.6 %copy.14 = bf16[2,64,128]{2,1,0:T(8,128)(2,1)} copy(bf16[2,64,128]{2,1,0:T(8,128)(2,1)S(1)} %copy-done) | data formatting | bytes 65536
Async XLA Ops:
  38.8 1.7 %copy-start = (bf16[2,64,128]{2,1,0:T(8,128)(2,1)S(1)}, bf16[2,64,128]{2,1,0:T(8,128)(2,1)}, u32[]{:S(2)}) copy-start(bf16[2,64,128]{2,1,0:T(8,128)(2,1)} %get-tuple-element.9) | copy-start | bytes 98308

commit v4 on v3

--- a/solution.py
+++ b/solution.py
@@ -7,7 +7,6 @@
 from jax.sharding import PartitionSpec as P
 
 FC_STEPS = 4
-LANES = 128
 MESH = pl.DeviceIdType.MESH
 VMEM_BYTES = 64 * 1024 * 1024
 F32 = jnp.float32
@@ -81,7 +80,7 @@
     small_all, refs = refs[:6], refs[6:]
     (
         variance_ref, matrix, forecast, anomaly, turned, cross_out, solved_turned, landing, chosen,
-        landing_turned, landing_cross, local_sem, send_l, recv_l, send_3, recv_3, send_s, recv_s,
+        landing_cross, local_sem, send_l, recv_l, send_3, recv_3, send_s, recv_s,
     ) = refs
     shift_ref, coupling_ref, cells_ref, weight_ref, reading_ref, jitter_ref = small_all
     lag, space = lax.axis_index("lag"), lax.axis_index("space")
@@ -89,18 +88,10 @@
     total = spaces * own
     cycles = variance_ref.shape[0]
     corners, wanted = cells_ref.shape[2], cells_ref.shape[3]
-    across = members // LANES
-    rows = own * across // lags
     member_rows = members // lags
 
-    def place(block):
-        return (
-            pl.ds(pl.multiple_of((block // across) * rows, rows), rows),
-            pl.ds(pl.multiple_of((block % across) * LANES, LANES), LANES),
-        )
-
     def member_place(block):
-        return (pl.ds(pl.multiple_of(block * member_rows, member_rows), member_rows),)
+        return pl.ds(pl.multiple_of(block * member_rows, member_rows), member_rows)
 
     def lag_at(step):
         return lax.rem(lag + step, lags)
@@ -135,10 +126,12 @@
         pl.semaphore_signal(barrier, inc=1, device_id=(lag_at(step), space), device_id_type=MESH)
     for step in range(1, spaces):
         pl.semaphore_signal(barrier, inc=1, device_id=(lag, space_at(step)), device_id_type=MESH)
+    local[0].wait()
+    turned[...] = slab_ref[...].astype(F32).T.astype(BF16)
     pl.semaphore_wait(barrier, lags - 1 + spaces - 1)
 
     scatter = [
-        send_lag(0, step, slab_hbm.at[place(lag_at(step))], landing.at[step])
+        send_lag(0, step, turned.at[member_place(lag_at(step))], landing.at[step])
         for step in range(1, lags)
     ]
     small = []
@@ -154,7 +147,7 @@
             )
             copy.start()
             small.append(copy)
-    for copy in local:
+    for copy in local[1:]:
         copy.wait()
     for copy in small:
         copy.wait()
@@ -197,22 +190,29 @@
         holds.append(hold_cycle)
         readings.append(jnp.concatenate(reading_cycle, axis=0))
 
-    source = slot_ref[0]
-    block = jnp.where(lag == source, slab_ref[place(lag)], jnp.zeros((rows, LANES), BF16))
+    source, target_0, target_1 = slot_ref[0], slot_ref[lags - 1], slot_ref[lags - 2]
+    mine = turned[member_place(lag)]
+    block = mine
     for step in range(1, lags):
         scatter[step - 1].wait_recv()
         block = jnp.where(lag_at(lags - step) == source, landing[step], block)
     chosen[...] = block
-    whole_ref[(space,) + place(lag)] = block
+    whole_ref[space, member_place(lag)] = block
     gather = [
-        send_lag(1, step, chosen, whole_ref.at[(space,) + place(lag)]) for step in range(1, lags)
+        send_lag(1, step, chosen, whole_ref.at[space, member_place(lag)])
+        for step in range(1, lags)
     ]
+    first, second = mine, mine
+    for step in range(1, lags):
+        sender = lag_at(lags - step)
+        first = jnp.where(sender == target_0, landing[step], first)
+        second = jnp.where(sender == target_1, landing[step], second)
     anomaly[...] = anomaly_of(slab_ref[...].astype(F32))
     forward = []
     for step in range(lags):
         if step:
             gather[step - 1].wait_recv()
-        spot = (space,) + place(lag_at(lags - step) if step else lag)
+        spot = (space, member_place(lag_at(lags - step) if step else lag))
         for aside in range(1, spaces):
             copy = pltpu.make_async_remote_copy(
                 src_ref=whole_ref.at[spot],
@@ -251,55 +251,55 @@
         forecast[...] = value
         return forecast[pl.ds(pl.multiple_of(space * own, own), own), :]
 
-    target_0, target_1 = slot_ref[lags - 1], slot_ref[lags - 2]
-
-    newest = whole_ref[...].reshape(total, members)
-    ahead = (dot(operator[0], newest) + dot(operator[1], newest)).astype(BF16)
+    def send_cross(cycle, cross):
+        cross_out[cycle] = cross.T.astype(BF16)
+        return [
+            send_lag(2 + cycle, step, cross_out.at[cycle], landing_cross.at[cycle, step])
+            for step in range(1, lags)
+        ]
+
+    def chosen_cross(cycle, target):
+        value = cross_out[cycle]
+        for step in range(1, lags):
+            value = jnp.where(lag_at(lags - step) == target, landing_cross[cycle, step], value)
+        return value
+
+    def retire(cycle, values, solved, cross):
+        solved_turned[cycle] = solved.astype(F32).T
+        weights = solved_turned[cycle, member_place(lag)].astype(BF16)
+        return (values.astype(F32) + dot(weights, cross)).astype(BF16)
+
+    newest = jnp.concatenate([whole_ref[part] for part in range(spaces)], axis=1)
+    ahead = (across_members(operator[0], newest) + across_members(operator[1], newest)).astype(BF16)
     spread, innovation = observed(0, ahead)
     cross = across_members(anomaly[...], spread)
+    crosses = send_cross(0, cross)
     ahead_f = ahead.astype(F32)
     cross_ahead = across_members(anomaly_of(ahead_f), spread)
-    solved = solve(0, spread, innovation)
-    updated = slab_ref[...].astype(F32) + dot_parts(cross, solved, 2)
-    turned[...] = updated.T.astype(BF16)
-    exchanged = [
-        send_lag(2, step, turned.at[member_place(lag_at(step))], landing_turned.at[step])
-        for step in range(1, lags)
-    ]
-    newest = (ahead_f + dot_parts(cross_ahead, solved, 2)).astype(BF16)
-    state = jnp.where(lag == target_0, own_rows(newest), updated.astype(BF16)).astype(F32)
+    solved_0 = solve(0, spread, innovation)
+    newest = (ahead_f + dot_parts(cross_ahead, solved_0, 2)).astype(BF16)
+    updated = (slab_ref[...].astype(F32) + dot_parts(cross, solved_0, 2)).astype(BF16)
+    state = jnp.where(lag == target_0, own_rows(newest), updated).astype(F32)
 
     ahead = (dot(operator[0], newest) + dot(operator[1], newest)).astype(BF16)
     spread, innovation = observed(1, ahead)
     cross = across_members(anomaly_of(state), spread)
-    cross_out[...] = cross.T.astype(BF16)
-    crosses = [
-        send_lag(3, step, cross_out, landing_cross.at[step]) for step in range(1, lags)
-    ]
+    crosses_1 = send_cross(1, cross)
     ahead_own = own_rows(ahead).astype(F32)
     cross_ahead = across_members(anomaly_of(ahead_own), spread)
-    solved = solve(1, spread, innovation)
+    solved_1 = solve(1, spread, innovation)
     base = jnp.where(lag == target_1, ahead_own, state)
     cross = jnp.where(lag == target_1, cross_ahead, cross)
-    out_ref[...] = (base + dot_parts(cross, solved, 2)).astype(BF16)
-    solved_turned[...] = solved.astype(F32).T
-
-    first = turned[member_place(lag)]
-    second = first
-    for step in range(1, lags):
-        exchanged[step - 1].wait_recv()
-        sender = lag_at(lags - step)
-        first = jnp.where(sender == target_0, landing_turned[step], first)
-        second = jnp.where(sender == target_1, landing_turned[step], second)
-    retired_ref[0] = first
-    cross_turned = cross_out[...]
-    for step in range(1, lags):
-        crosses[step - 1].wait_recv()
-        sender = lag_at(lags - step)
-        cross_turned = jnp.where(sender == target_1, landing_cross[step], cross_turned)
-    mine = solved_turned[member_place(lag)].astype(BF16)
-    retired_ref[1] = (second.astype(F32) + dot(mine, cross_turned)).astype(BF16)
-    for copy in scatter + gather + forward + exchanged + crosses:
+    out_ref[...] = (base + dot_parts(cross, solved_1, 2)).astype(BF16)
+
+    for copy in crosses:
+        copy.wait_recv()
+    retired_ref[0] = retire(0, first, solved_0, chosen_cross(0, target_0))
+    second = retire(0, second, solved_0, chosen_cross(0, target_1))
+    for copy in crosses_1:
+        copy.wait_recv()
+    retired_ref[1] = retire(1, second, solved_1, chosen_cross(1, target_1))
+    for copy in scatter + gather + forward + crosses + crosses_1:
         copy.wait_send()
 
 
@@ -310,7 +310,6 @@
     slab = ensemble[0]
     own, members = slab.shape
     cycles, count = observation_variance.shape
-    rows = own * (members // LANES) // lags
     member_rows = members // lags
     total = spaces * own
     smem = pl.BlockSpec(memory_space=pltpu.SMEM)
@@ -331,7 +330,7 @@
         out_specs=[vmem] * 2,
         scratch_shapes=[
             pltpu.VMEM((own, members), BF16),
-            pltpu.VMEM((spaces, own, members), BF16),
+            pltpu.VMEM((spaces, members, own), BF16),
         ]
         + [pltpu.VMEM((spaces,) + a.shape, a.dtype) for a in small]
         + [
@@ -340,12 +339,11 @@
             pltpu.VMEM((total, members), BF16),
             pltpu.VMEM((own, members), BF16),
             pltpu.VMEM((members, own), BF16),
-            pltpu.VMEM((count, own), BF16),
-            pltpu.VMEM((members, count), F32),
-            pltpu.VMEM((lags, rows, LANES), BF16),
-            pltpu.VMEM((rows, LANES), BF16),
+            pltpu.VMEM((cycles, count, own), BF16),
+            pltpu.VMEM((cycles, members, count), F32),
             pltpu.VMEM((lags, member_rows, own), BF16),
-            pltpu.VMEM((lags, count, own), BF16),
+            pltpu.VMEM((member_rows, own), BF16),
+            pltpu.VMEM((cycles, lags, count, own), BF16),
             dma((8,)),
             dma((4, lags)), dma((4, lags)),
             dma((lags, spaces)), dma((lags, spaces)),

time: 41.3 us -> 38.1 us (0.923)
  Pallas kernels: 38.2 us -> 34.7 us
    pallas_call x1, Pallas kernels: 38.2 us -> 34.7 us  [on_device(): pl.pallas_call(functools.partial(smoother_kernel, lags, spaces), out_shap...]
where the time goes in v4:
time: 38.1 us; the launch traced here: 37.6 us
  Pallas kernels  34.7 us (91%)
  local copies, waits for them, and re-layouts  2.29 us (6%)
  between operations  0.65 us (2%)
    pallas_call x1, Pallas kernels, on_device(): pl.pallas_call(functools.partial(smoother_kernel, lags, spaces), out_shap...  34.7 us
    unnamed x4, local copies, waits for them, and re-layouts  2.29 us

profile of v4, /device:TPU:1, one launch (start us, length us, event | category | flops | bytes accessed | tf_op | source)
XLA Modules:
  0.0 37.6 jit_solution(14201496750029135009)
XLA Ops:
  0.6 34.7 %smoother.1 = (bf16[128,1024]{1,0:T(8,128)(2,1)}, bf16[2,64,128]{2,1,0:T(8,128)(2,1)}) custom-call(s32[16]{0:T(128)} %slot_ref.1, bf16[128,1024]{1,0:T(8,128)(2,1)} %bitcast.2, f32[2,32]{1,0:T(2,128)} %variance_hbm.1, s32[6,128]{1,0:T(8,128)} %refs_0_.1, f32[6,128]{1,0:T(8,128)} %refs_1_.1, s32[2,4,16]{2,1,0:T(4,128)} %refs_2_.1, f32[2,4,16]{2,1,0:T(4,128)} %refs_3_.1, ...), custom_call_target="tpu_custom_call" | custom-call | tf_op jit(solution)/shard_map/smoother/pallas_call | solution.py:323
  35.3 0.0 copy-start
  35.3 1.7 %copy.13 = bf16[1,128,1024]{2,1,0:T(8,128)(2,1)} copy(bf16[1,128,1024]{2,1,0:T(8,128)(2,1)} %bitcast.3) | data formatting | bytes 524288
  37.0 0.0 copy-done
  37.0 0.6 %copy.14 = bf16[2,64,128]{2,1,0:T(8,128)(2,1)} copy(bf16[2,64,128]{2,1,0:T(8,128)(2,1)S(1)} %copy-done) | data formatting | bytes 65536
Async XLA Ops:
  35.3 1.7 %copy-start = (bf16[2,64,128]{2,1,0:T(8,128)(2,1)S(1)}, bf16[2,64,128]{2,1,0:T(8,128)(2,1)}, u32[]{:S(2)}) copy-start(bf16[2,64,128]{2,1,0:T(8,128)(2,1)} %get-tuple-element.9) | copy-start | bytes 98308

commit v5 on v4

--- a/solution.py
+++ b/solution.py
@@ -79,7 +79,7 @@
     out_ref, retired_ref, slab_ref, whole_ref, refs = refs[0], refs[1], refs[2], refs[3], refs[4:]
     small_all, refs = refs[:6], refs[6:]
     (
-        variance_ref, matrix, forecast, anomaly, turned, cross_out, solved_turned, landing, chosen,
+        variance_ref, matrix, forecast, anomaly, turned, cross_out, solved_turned, landing,
         landing_cross, local_sem, send_l, recv_l, send_3, recv_3, send_s, recv_s,
     ) = refs
     shift_ref, coupling_ref, cells_ref, weight_ref, reading_ref, jitter_ref = small_all
@@ -196,27 +196,36 @@
     for step in range(1, lags):
         scatter[step - 1].wait_recv()
         block = jnp.where(lag_at(lags - step) == source, landing[step], block)
-    chosen[...] = block
     whole_ref[space, member_place(lag)] = block
-    gather = [
-        send_lag(1, step, chosen, whole_ref.at[space, member_place(lag)])
-        for step in range(1, lags)
-    ]
-    first, second = mine, mine
-    for step in range(1, lags):
-        sender = lag_at(lags - step)
-        first = jnp.where(sender == target_0, landing[step], first)
-        second = jnp.where(sender == target_1, landing[step], second)
-    anomaly[...] = anomaly_of(slab_ref[...].astype(F32))
+
+    inner = 4 if lags % 4 == 0 else 1
+    outers = lags // inner
+    outer, within = lag // inner, lag % inner
+
+    def lag_near(far, near):
+        return lax.rem(outer + far, outers) * inner + lax.rem(within + near, inner)
+
+    def hand_on(far, near, position, to):
+        spot = whole_ref.at[space, member_place(position)]
+        copy = pltpu.make_async_remote_copy(
+            src_ref=spot,
+            dst_ref=spot,
+            send_sem=send_l.at[1, far * inner + near],
+            recv_sem=recv_l.at[1, far * inner + near],
+            device_id=(to, space),
+            device_id_type=MESH,
+        )
+        copy.start()
+        gather[far, near] = copy
+
     forward = []
-    for step in range(lags):
-        if step:
-            gather[step - 1].wait_recv()
-        spot = (space, member_place(lag_at(lags - step) if step else lag))
+
+    def across_spaces(step, position):
+        spot = whole_ref.at[space, member_place(position)]
         for aside in range(1, spaces):
             copy = pltpu.make_async_remote_copy(
-                src_ref=whole_ref.at[spot],
-                dst_ref=whole_ref.at[spot],
+                src_ref=spot,
+                dst_ref=spot,
                 send_sem=send_3.at[step, aside],
                 recv_sem=recv_3.at[step, aside],
                 device_id=(lag, space_at(aside)),
@@ -224,6 +233,29 @@
             )
             copy.start()
             forward.append(copy)
+
+    gather = {}
+    for far in range(1, outers):
+        hand_on(far, 0, lag, lag_near(far, 0))
+    for near in range(1, inner):
+        hand_on(0, near, lag, lag_near(0, near))
+    across_spaces(0, lag)
+    first, second = mine, mine
+    for step in range(1, lags):
+        sender = lag_at(lags - step)
+        first = jnp.where(sender == target_0, landing[step], first)
+        second = jnp.where(sender == target_1, landing[step], second)
+    anomaly[...] = anomaly_of(slab_ref[...].astype(F32))
+    for far in range(1, outers):
+        gather[far, 0].wait_recv()
+        position = lag_near(outers - far, 0)
+        for near in range(1, inner):
+            hand_on(far, near, position, lag_near(0, near))
+        across_spaces(far * inner, position)
+    for far in range(outers):
+        for near in range(1, inner):
+            gather[far, near].wait_recv()
+            across_spaces(far * inner + near, lag_near(outers - far, inner - near))
     for copy in forward:
         copy.wait_recv()
 
@@ -299,8 +331,19 @@
     for copy in crosses_1:
         copy.wait_recv()
     retired_ref[1] = retire(1, second, solved_1, chosen_cross(1, target_1))
-    for copy in scatter + gather + forward + crosses + crosses_1:
+    for copy in scatter + list(gather.values()) + forward + crosses + crosses_1:
         copy.wait_send()
+
+
+def keep_kernel(analysed_ref, retired_ref, analysed_out, retired_out, sems):
+    copies = [
+        pltpu.make_async_copy(analysed_ref, analysed_out, sems.at[0]),
+        pltpu.make_async_copy(retired_ref, retired_out, sems.at[1]),
+    ]
+    for copy in copies:
+        copy.start()
+    for copy in copies:
+        copy.wait()
 
 
 def on_device(
@@ -342,7 +385,6 @@
             pltpu.VMEM((cycles, count, own), BF16),
             pltpu.VMEM((cycles, members, count), F32),
             pltpu.VMEM((lags, member_rows, own), BF16),
-            pltpu.VMEM((member_rows, own), BF16),
             pltpu.VMEM((cycles, lags, count, own), BF16),
             dma((8,)),
             dma((4, lags)), dma((4, lags)),
@@ -354,6 +396,18 @@
         ),
         name="smoother",
     )(slot_order, slab, observation_variance, *small)
+    analysed, retired = pl.pallas_call(
+        keep_kernel,
+        out_shape=[
+            jax.ShapeDtypeStruct(analysed.shape, BF16),
+            jax.ShapeDtypeStruct(retired.shape, BF16),
+        ],
+        in_specs=[hbm] * 2,
+        out_specs=[hbm] * 2,
+        scratch_shapes=[dma((2,))],
+        compiler_params=pltpu.CompilerParams(vmem_limit_bytes=VMEM_BYTES),
+        name="keep",
+    )(analysed, retired)
     return analysed[None], retired
 
 

time: 38.1 us -> 45.1 us (1.18)
  Pallas kernels: 34.7 us -> 44.3 us
  local copies, waits for them, and re-layouts: 2.29 us -> 0 us
    pallas_call x0 -> x1, Pallas kernels: none -> 10.1 us  [on_device(): pl.pallas_call(keep_kernel, out_shape=[jax.ShapeDtypeStruct(analysed.shap...]
    unnamed x4 -> x0, local copies, waits for them, and re-layouts: 2.29 us -> none
where the time goes in v5:
time: 45.1 us; the launch traced here: 44.9 us
  Pallas kernels  44.3 us (98%)
  between operations  0.64 us (1%)
    pallas_call x1, Pallas kernels, on_device(): pl.pallas_call(functools.partial(smoother_kernel, lags, spaces), out_shap...  34.3 us
    pallas_call x1, Pallas kernels, on_device(): pl.pallas_call(keep_kernel, out_shape=[jax.ShapeDtypeStruct(analysed.shap...  10.1 us

profile of v5, /device:TPU:1, one launch (start us, length us, event | category | flops | bytes accessed | tf_op | source)
XLA Modules:
  0.0 44.9 jit_solution(18199473636753876419)
XLA Ops:
  0.6 34.3 %smoother.1 = (bf16[128,1024]{1,0:T(8,128)(2,1)}, bf16[2,64,128]{2,1,0:T(8,128)(2,1)}) custom-call(s32[16]{0:T(128)} %slot_ref.1, bf16[128,1024]{1,0:T(8,128)(2,1)} %bitcast.2, f32[2,32]{1,0:T(2,128)} %variance_hbm.1, s32[6,128]{1,0:T(8,128)} %refs_0_.1, f32[6,128]{1,0:T(8,128)} %refs_1_.1, s32[2,4,16]{2,1,0:T(4,128)} %refs_2_.1, f32[2,4,16]{2,1,0:T(4,128)} %refs_3_.1, ...), custom_call_target="tpu_custom_call" | custom-call | tf_op jit(solution)/shard_map/smoother/pallas_call | solution.py:366
  34.9 10.1 %keep.1 = (bf16[128,1024]{1,0:T(8,128)(2,1)}, bf16[2,64,128]{2,1,0:T(8,128)(2,1)}) custom-call(bf16[128,1024]{1,0:T(8,128)(2,1)} %get-tuple-element.6.analysed_ref, bf16[2,64,128]{2,1,0:T(8,128)(2,1)} %get-tuple-element.7.retired_ref), custom_call_target="tpu_custom_call" | custom-call | tf_op jit(solution)/shard_map/keep/pallas_call | solution.py:399

commit v6 on v5

--- a/solution.py
+++ b/solution.py
@@ -335,15 +335,9 @@
         copy.wait_send()
 
 
-def keep_kernel(analysed_ref, retired_ref, analysed_out, retired_out, sems):
-    copies = [
-        pltpu.make_async_copy(analysed_ref, analysed_out, sems.at[0]),
-        pltpu.make_async_copy(retired_ref, retired_out, sems.at[1]),
-    ]
-    for copy in copies:
-        copy.start()
-    for copy in copies:
-        copy.wait()
+def keep_kernel(analysed_ref, retired_ref, analysed_out, retired_out):
+    analysed_out[...] = analysed_ref[...]
+    retired_out[...] = retired_ref[...]
 
 
 def on_device(
@@ -402,9 +396,8 @@
             jax.ShapeDtypeStruct(analysed.shape, BF16),
             jax.ShapeDtypeStruct(retired.shape, BF16),
         ],
-        in_specs=[hbm] * 2,
-        out_specs=[hbm] * 2,
-        scratch_shapes=[dma((2,))],
+        in_specs=[vmem] * 2,
+        out_specs=[vmem] * 2,
         compiler_params=pltpu.CompilerParams(vmem_limit_bytes=VMEM_BYTES),
         name="keep",
     )(analysed, retired)

time: 45.1 us -> 36.7 us (0.81)
  Pallas kernels: 44.3 us -> 35.9 us
    pallas_call x1, Pallas kernels: 10.1 us -> 1.68 us  [on_device(): pl.pallas_call(keep_kernel, out_shape=[jax.ShapeDtypeStruct(analysed.shap...]
where the time goes in v6:
time: 36.7 us; the launch traced here: 36.6 us
  Pallas kernels  35.9 us (98%)
  between operations  0.64 us (2%)
    pallas_call x1, Pallas kernels, on_device(): pl.pallas_call(functools.partial(smoother_kernel, lags, spaces), out_shap...  34.3 us
    pallas_call x1, Pallas kernels, on_device(): pl.pallas_call(keep_kernel, out_shape=[jax.ShapeDtypeStruct(analysed.shap...  1.68 us

profile of v6, /device:TPU:1, one launch (start us, length us, event | category | flops | bytes accessed | tf_op | source)
XLA Modules:
  0.0 36.6 jit_solution(4620554347982765731)
XLA Ops:
  0.6 34.3 %smoother.1 = (bf16[128,1024]{1,0:T(8,128)(2,1)}, bf16[2,64,128]{2,1,0:T(8,128)(2,1)}) custom-call(s32[16]{0:T(128)} %slot_ref.1, bf16[128,1024]{1,0:T(8,128)(2,1)} %bitcast.2, f32[2,32]{1,0:T(2,128)} %variance_hbm.1, s32[6,128]{1,0:T(8,128)} %refs_0_.1, f32[6,128]{1,0:T(8,128)} %refs_1_.1, s32[2,4,16]{2,1,0:T(4,128)} %refs_2_.1, f32[2,4,16]{2,1,0:T(4,128)} %refs_3_.1, ...), custom_call_target="tpu_custom_call" | custom-call | tf_op jit(solution)/shard_map/smoother/pallas_call | solution.py:360
  34.9 1.7 %keep.1 = (bf16[128,1024]{1,0:T(8,128)(2,1)}, bf16[2,64,128]{2,1,0:T(8,128)(2,1)}) custom-call(bf16[128,1024]{1,0:T(8,128)(2,1)} %get-tuple-element.6.analysed_ref, bf16[2,64,128]{2,1,0:T(8,128)(2,1)} %get-tuple-element.7.retired_ref), custom_call_target="tpu_custom_call" | custom-call | tf_op jit(solution)/shard_map/keep/pallas_call | solution.py:393
